TPU v7x, 256 devices: a whole 4x4x8 slice. The times are simulated.
256 devices in a mesh: seq: 8 (over x, core), mp: 32 (over y, z).
Axes of the slice: x: 4, y: 4, z: 8, core: 2. Of those that a mesh axis runs over, the one named last changes fastest.
Arguments:
- inputs: bfloat16 [1024, 12288], P('seq'), may hold values from -6 to 6
- out_grads: bfloat16 [1024, 12288], P('seq'), may hold values from -6 to 6
- w1_blocks: bfloat16 [192, 32, 128, 128], P('mp', 'seq'), may hold values from -0.109375 to 0.109375
- w1_rows: int32 [192, 32], P('mp', 'seq'), may hold values from 0 to 95, as said below
- w1_count: int32 [192], P('mp'), may hold values from 16 to 32, as said below
- w2_blocks: bfloat16 [192, 32, 128, 128], P('mp', 'seq'), may hold values from -0.109375 to 0.109375
- w2_cols: int32 [192, 32], P('mp', 'seq'), may hold values from 0 to 95, as said below
- w2_count: int32 [192], P('mp'), may hold values from 16 to 32, as said below
Outputs:
- input_grads: bfloat16 [1024, 12288], P('seq', 'mp')
- w1_grads: bfloat16 [192, 32, 128, 128], P('mp', 'seq')
- w2_grads: bfloat16 [192, 32, 128, 128], P('mp', 'seq')
Inputs may be any that keep to these rules, and one draw needn't show every extreme that they name: `w1_rows`: in each hidden block column the 32 entries name distinct block rows; only the first w1_count entries are live. `w1_count`: some hidden block column holds 32 live blocks and some 32 // 2. `w2_cols`: in each hidden block row the 32 entries name distinct block columns; only the first w2_count entries are live. `w2_count`: some hidden block row holds 32 live blocks and some 32 // 2.
All inputs are finite; a program needn't handle non-finite values.
Results may differ from a plain program's by a relative error of at most 0.005.
Values may be sent and summed in bfloat16 or wider, within the bound.
A program may use at most 192 MiB of HBM per device.

v0:
```python
import jax
import jax.numpy as jnp
from jax import lax
from jax.experimental import pallas as pl
from jax.experimental.pallas import tpu as pltpu
from jax.sharding import PartitionSpec as P

GELU_C = 0.7978845608028654
CUBIC = 0.044715
BF16 = jnp.bfloat16
F32 = jnp.float32
MESH = pl.DeviceIdType.MESH
NT = (((1,), (1,)), ((), ()))

NX = 4
NY = 4
NZ = 8
COLS = 3
D_ORDER = (2, 1, 3, 0)


def gelu_both(h):
    arg = GELU_C * (h + CUBIC * h * h * h)
    t = jnp.tanh(arg)
    value = 0.5 * h * (1.0 + t)
    slope = 0.5 * (1.0 + t) + 0.5 * h * (1.0 - t * t) * GELU_C * (1.0 + 3.0 * CUBIC * h * h)
    return value, slope


def kernel(
    x_hbm, dy_hbm, w1_hbm, w2_hbm, pkt_hbm,
    dx_out, g1_out, g2_out,
    stx, sty, xf, dyf, w1a, w1b, w1c, w2a, w2b, w2c,
    idxv, invv, idx_sm, inv_sm,
    ghcat, ght, actt,
    d1a, d1b, d1c, d2a, d2b, d2c,
    r1, r2, rl1, rl2, rr1, rr2, rp1, rp2,
    dxo, pxs, prx, yrc, zs, zown, zrc,
    loc_sem, pk_s, pk_r, xs_s, xs_r, wd_s, wd_r, wp_s, wp_r, wf_s, wf_r,
    s1_s, s1_r, s2_s, s2_r, sp_s, sp_r, px_s, px_r, y_s, y_r, z_s, z_r,
):
    w1 = (w1a, w1b, w1c)
    w2 = (w2a, w2b, w2c)
    d1 = (d1a, d1b, d1c)
    d2 = (d2a, d2b, d2c)
    s = lax.axis_index("seq")
    m = lax.axis_index("mp")
    x = s // 2
    c = s % 2
    o = 1 - c
    xl = (x + 3) % 4
    xr = (x + 1) % 4
    xo = (x + 2) % 4
    y = m // NZ
    z = m % NZ
    pending = []

    def send(src, dst, ssem, rsem, dev):
        cp = pltpu.make_async_remote_copy(
            src_ref=src, dst_ref=dst, send_sem=ssem, recv_sem=rsem,
            device_id=dev, device_id_type=MESH,
        )
        cp.start()
        pending.append(cp)

    def arrived(ref, ssem, rsem):
        pltpu.make_async_remote_copy(
            src_ref=ref, dst_ref=ref, send_sem=ssem, recv_sem=rsem,
            device_id=(s, m), device_id_type=MESH,
        ).wait_recv()

    local = [
        pltpu.make_async_copy(x_hbm, stx, loc_sem.at[0]),
        pltpu.make_async_copy(dy_hbm, sty, loc_sem.at[1]),
        pltpu.make_async_copy(pkt_hbm, idxv.at[s], loc_sem.at[2]),
    ]
    wlocal = []
    for j in range(COLS):
        wlocal.append(
            (
                pltpu.make_async_copy(
                    w1_hbm.at[3 * c + j], w1[j].at[pl.ds(4 * s, 4)], loc_sem.at[3 + 2 * j]),
                pltpu.make_async_copy(
                    w2_hbm.at[3 * c + j], w2[j].at[pl.ds(4 * s, 4)], loc_sem.at[4 + 2 * j]),
            )
        )
    for cp in local:
        cp.start()
    for pair in wlocal:
        for cp in pair:
            cp.start()

    barrier = pltpu.get_barrier_semaphore()
    for e in range(1, 8):
        pl.semaphore_signal(barrier, inc=1, device_id=((s + e) % 8, m), device_id_type=MESH)
    for e in range(1, NY):
        pl.semaphore_signal(
            barrier, inc=1, device_id=(s, ((y + e) % NY) * NZ + z), device_id_type=MESH)
    for e in range(1, NZ):
        pl.semaphore_signal(
            barrier, inc=1, device_id=(s, y * NZ + (z + e) % NZ), device_id_type=MESH)
    pl.semaphore_wait(barrier, 7 + NY - 1 + NZ - 1)

    for e in range(1, 8):
        send(pkt_hbm, idxv.at[s], pk_s.at[e - 1], pk_r.at[e - 1], ((s + e) % 8, m))

    def direct(j):
        for w, (src, dst) in enumerate(((w1_hbm, w1[j]), (w2_hbm, w2[j]))):
            for way, xd in ((0, xr), (1, xl)):
                for cd in range(2):
                    send(
                        src.at[3 * cd + j], dst.at[pl.ds(4 * s, 4)],
                        wd_s.at[j, w, way, cd], wd_r.at[j, w, way, c], (xd * 2 + cd, m),
                    )
            send(
                src.at[3 * o + j], dst.at[pl.ds(4 * s, 4)],
                wp_s.at[j, w], wp_r.at[j, w], (x * 2 + o, m),
            )

    def from_neighbour(j, w, way):
        dst = (w1, w2)[w][j]
        xs = (xl, xr)[way]
        for cs in range(2):
            arrived(dst.at[pl.ds(8 * xs + 4 * cs, 4)], wd_s.at[j, w, way, cs], wd_r.at[j, w, way, cs])

    def forward(j):
        from_neighbour(j, 0, 0)
        send(w1[j].at[pl.ds(8 * xl, 8)], w1[j].at[pl.ds(8 * xl, 8)],
             wf_s.at[j, 0], wf_r.at[j, 0], (xr * 2 + c, m))
        from_neighbour(j, 1, 1)
        send(w2[j].at[pl.ds(8 * xr, 8)], w2[j].at[pl.ds(8 * xr, 8)],
             wf_s.at[j, 1], wf_r.at[j, 1], (xl * 2 + c, m))

    def complete(j):
        for cp in wlocal[j]:
            cp.wait()
        for w in range(2):
            arrived((w1, w2)[w][j].at[pl.ds(8 * x + 4 * o, 4)], wp_s.at[j, w], wp_r.at[j, w])
        from_neighbour(j, 0, 1)
        from_neighbour(j, 1, 0)
        for w in range(2):
            arrived((w1, w2)[w][j].at[pl.ds(8 * xo, 8)], wf_s.at[j, w], wf_r.at[j, w])

    direct(0)
    for at, (flat, full) in enumerate(((stx, xf), (sty, dyf))):
        local[at].wait()

        def regroup(r, carry):
            full[r, 0:128] = flat[:, pl.ds(pl.multiple_of(r * 128, 128), 128)]
            return carry

        lax.fori_loop(0, 96, regroup, 0)
        send(full.at[:, pl.ds(0, 128)], full.at[:, pl.ds(128, 128)],
             xs_s.at[at], xs_r.at[at], (x * 2 + o, m))
    direct(1)

    for j in range(COLS):
        w1[j][32] = jnp.zeros((128, 128), BF16)

    local[2].wait()
    for e in range(1, 8):
        arrived(idxv.at[(s + 8 - e) % 8], pk_s.at[e - 1], pk_r.at[e - 1])
    total = idxv[0, 8:16]
    for t in range(1, 8):
        total = total + idxv[t, 8:16]
    invv[...] = jnp.where(total > 0, total - 1, 32)
    to_sm = pltpu.make_async_copy(idxv, idx_sm, loc_sem.at[9])
    to_sm2 = pltpu.make_async_copy(invv, inv_sm, loc_sem.at[10])
    to_sm.start()
    to_sm2.start()
    to_sm.wait()
    to_sm2.wait()

    def picked(ref, who, col, first):
        return jnp.concatenate([ref[idx_sm[who, col, first + u]] for u in range(4)], axis=1)

    def forward_pass(j):
        col = 3 * c + j

        def body(p, carry):
            h, a = carry
            xs = picked(xf, p, col, 0)
            ws = w1[j][pl.ds(4 * p, 4)].reshape(512, 128)
            h = h + jnp.dot(xs, ws, preferred_element_type=F32)
            ys = picked(dyf, p, col, 4)
            vs = jnp.concatenate([w2[j][4 * p + u] for u in range(4)], axis=1)
            a = a + lax.dot_general(ys, vs, NT, preferred_element_type=F32)
            return h, a

        zero = jnp.zeros((256, 128), F32)
        h, a = lax.fori_loop(0, 8, body, (zero, zero))
        value, slope = gelu_both(h)
        grad = a * slope
        ghcat[:, j * 128:(j + 1) * 128] = grad.astype(BF16)
        ght[j] = grad.T.astype(BF16)
        actt[j] = value.T.astype(BF16)

    def weight_grads(j):
        col = 3 * c + j

        def body(q, carry):
            who = (2 * xo + q) % 8
            t1 = jnp.dot(ght[j], picked(xf, who, col, 0), preferred_element_type=F32)
            t2 = jnp.dot(actt[j], picked(dyf, who, col, 4), preferred_element_type=F32)
            for u in range(4):
                d1[j][4 * who + u] = t1[:, 128 * u:128 * (u + 1)].astype(BF16)
                d2[j][4 * who + u] = t2[:, 128 * u:128 * (u + 1)].astype(BF16)
            return carry

        lax.fori_loop(0, 8, body, 0)

    def stage_one(j):
        send(d1[j].at[pl.ds(8 * xo, 8)], r1.at[j], s1_s.at[j, 0], s1_r.at[j, 0], (xr * 2 + c, m))
        send(d2[j].at[pl.ds(8 * xo, 8)], r2.at[j], s1_s.at[j, 1], s1_r.at[j, 1], (xl * 2 + c, m))

    def stage_two_plain(j):
        col = 3 * c + j
        for co in range(2):
            send(d2[j].at[pl.ds(8 * xr + 4 * co, 4)], rl2.at[col],
                 s2_s.at[j, 1, 0, co], s2_r.at[1, 0, col], (xr * 2 + co, m))
            send(d1[j].at[pl.ds(8 * xl + 4 * co, 4)], rr1.at[col],
                 s2_s.at[j, 0, 1, co], s2_r.at[0, 1, col], (xl * 2 + co, m))
        send(d1[j].at[pl.ds(8 * x + 4 * o, 4)], rp1.at[j], sp_s.at[j, 0], sp_r.at[j, 0], (x * 2 + o, m))
        send(d2[j].at[pl.ds(8 * x + 4 * o, 4)], rp2.at[j], sp_s.at[j, 1], sp_r.at[j, 1], (x * 2 + o, m))

    def stage_two_added(j):
        col = 3 * c + j
        arrived(r1.at[j], s1_s.at[j, 0], s1_r.at[j, 0])

        def add1(k, carry):
            at = 8 * xr + k
            d1[j][at] = (d1[j][at].astype(F32) + r1[j, k].astype(F32)).astype(BF16)
            return carry

        lax.fori_loop(0, 8, add1, 0)
        for co in range(2):
            send(d1[j].at[pl.ds(8 * xr + 4 * co, 4)], rl1.at[col],
                 s2_s.at[j, 0, 0, co], s2_r.at[0, 0, col], (xr * 2 + co, m))
        arrived(r2.at[j], s1_s.at[j, 1], s1_r.at[j, 1])

        def add2(k, carry):
            at = 8 * xl + k
            d2[j][at] = (d2[j][at].astype(F32) + r2[j, k].astype(F32)).astype(BF16)
            return carry

        lax.fori_loop(0, 8, add2, 0)
        for co in range(2):
            send(d2[j].at[pl.ds(8 * xl + 4 * co, 4)], rr2.at[col],
                 s2_s.at[j, 1, 1, co], s2_r.at[1, 1, col], (xl * 2 + co, m))

    def finish(j):
        for cc, own in ((c, True), (o, False)):
            col = 3 * cc + j
            arrived(rr1.at[col], s2_s.at[j, 0, 1, 0], s2_r.at[0, 1, col])
            arrived(rl2.at[col], s2_s.at[j, 1, 0, 0], s2_r.at[1, 0, col])
            arrived(rl1.at[col], s2_s.at[j, 0, 0, 0], s2_r.at[0, 0, col])
            arrived(rr2.at[col], s2_s.at[j, 1, 1, 0], s2_r.at[1, 1, col])
            if not own:
                arrived(rp1.at[j], sp_s.at[j, 0], sp_r.at[j, 0])
                arrived(rp2.at[j], sp_s.at[j, 1], sp_r.at[j, 1])

            def body(k, carry):
                mine1 = d1[j][4 * s + k] if own else rp1[j, k]
                mine2 = d2[j][4 * s + k] if own else rp2[j, k]
                t1 = mine1.astype(F32) + rl1[col, k].astype(F32) + rr1[col, k].astype(F32)
                t2 = mine2.astype(F32) + rl2[col, k].astype(F32) + rr2[col, k].astype(F32)
                g1_out[col, k] = t1.T.astype(BF16)
                g2_out[col, k] = t2.astype(BF16)
                return carry

            lax.fori_loop(0, 4, body, 0)

    def input_chunk(d):
        yy = (y + d) % NY

        def body(q, carry):
            zz = (z + q + 1) % NZ
            base = (yy * NZ + zz) * 3
            rows = []
            for t in range(3):
                rows.append(
                    jnp.concatenate(
                        [w1[j][inv_sm[3 * c + j, base + t]] for j in range(COLS)], axis=1))
            rhs = jnp.concatenate(rows, axis=0)
            out = lax.dot_general(ghcat[...], rhs, NT, preferred_element_type=F32)
            dxo[d, q] = out[:128]
            pxs[d, q] = out[128:].astype(BF16)
            return carry

        lax.fori_loop(0, NZ, body, 0)
        send(pxs.at[d], prx.at[d], px_s.at[d], px_r.at[d], (x * 2 + o, m))

    def input_pair(d):
        arrived(prx.at[d], px_s.at[d], px_r.at[d])

        def body(q, carry):
            both = dxo[d, q] + prx[d, q].astype(F32)
            if d:
                prx[d, q] = both.astype(BF16)
            else:
                dxo[d, q] = both
            return carry

        if d:
            for half in range(2):
                lax.fori_loop(4 * half, 4 * half + 4, body, 0)
                send(prx.at[d, pl.ds(4 * half, 4)], yrc.at[d - 1, pl.ds(4 * half, 4)],
                     y_s.at[d - 1, half], y_r.at[d - 1, half], (s, ((y + d) % NY) * NZ + z))
        else:
            lax.fori_loop(0, NZ, body, 0)

    def input_sum(half):
        for d in range(1, NY):
            arrived(yrc.at[d - 1, pl.ds(4 * half, 4)], y_s.at[d - 1, half], y_r.at[d - 1, half])
        for q in range(4 * half, 4 * half + 4):
            both = dxo[0, q]
            for d in range(1, NY):
                both = both + yrc[d - 1, q].astype(F32)
            if q < NZ - 1:
                zs[q] = both.astype(BF16)
                send(zs.at[q], zrc.at[q], z_s.at[q], z_r.at[q], (s, y * NZ + (z + q + 1) % NZ))
            else:
                zown[...] = both

    forward(0)
    direct(2)
    forward(1)
    arrived(xf.at[:, pl.ds(128, 128)], xs_s.at[0], xs_r.at[0])
    arrived(dyf.at[:, pl.ds(128, 128)], xs_s.at[1], xs_r.at[1])
    complete(0)
    forward_pass(0)
    forward(2)
    complete(1)
    forward_pass(1)
    weight_grads(0)
    weight_grads(1)
    complete(2)
    stage_one(0)
    stage_one(1)
    forward_pass(2)
    input_chunk(D_ORDER[0])
    input_chunk(D_ORDER[1])
    input_pair(D_ORDER[0])
    input_chunk(D_ORDER[2])
    input_pair(D_ORDER[1])
    input_chunk(D_ORDER[3])
    input_pair(D_ORDER[2])
    stage_two_plain(0)
    stage_two_plain(1)
    weight_grads(2)
    stage_one(2)
    stage_two_plain(2)
    input_pair(D_ORDER[3])
    stage_two_added(0)
    stage_two_added(1)
    stage_two_added(2)
    input_sum(0)
    input_sum(1)
    finish(0)
    finish(1)
    for q in range(NZ - 1):
        arrived(zrc.at[q], z_s.at[q], z_r.at[q])
    whole = zown[...]
    for q in range(NZ - 1):
        whole = whole + zrc[q].astype(F32)
    dx_out[...] = whole.astype(BF16)
    finish(2)
    for cp in pending:
        cp.wait_send()


def per_device(inputs, out_grads, w1_blocks, w1_rows, w1_count, w2_blocks, w2_cols, w2_count):
    s = lax.axis_index("seq")
    own_ids = s * 4 + jnp.arange(4, dtype=jnp.int32)
    live_one = (own_ids[None, :] < w1_count[:, None])[:, :, None, None]
    live_two = (own_ids[None, :] < w2_count[:, None])[:, :, None, None]
    nothing = jnp.zeros((), BF16)
    w1m = jnp.where(live_one, w1_blocks, nothing)
    w2m = jnp.where(live_two, w2_blocks, nothing)
    lanes = jnp.arange(128, dtype=jnp.int32)
    slot_of = jnp.sum(
        jnp.where(w1_rows[:, :, None] == lanes[None, None, :], own_ids[None, :, None] + 1, 0), axis=1)
    named = jnp.concatenate([w1_rows, w2_cols], axis=1)
    packet = jnp.concatenate(
        [jnp.pad(named, ((0, 2), (0, 120))), jnp.pad(slot_of, ((0, 2), (0, 0)))], axis=0)

    any_space = pl.BlockSpec(memory_space=pl.ANY)
    vmem = pl.BlockSpec(memory_space=pltpu.VMEM)
    dma = pltpu.SemaphoreType.DMA
    w_scratch = [pltpu.VMEM((33, 128, 128), BF16)] * 3 + [pltpu.VMEM((32, 128, 128), BF16)] * 3
    d_scratch = [pltpu.VMEM((32, 128, 128), BF16)] * 6
    dx, g1, g2 = pl.pallas_call(
        kernel,
        out_shape=(
            jax.ShapeDtypeStruct((128, 384), BF16),
            jax.ShapeDtypeStruct((6, 4, 128, 128), BF16),
            jax.ShapeDtypeStruct((6, 4, 128, 128), BF16),
        ),
        in_specs=[any_space] * 5,
        out_specs=(vmem, vmem, vmem),
        scratch_shapes=[
            pltpu.VMEM((128, 12288), BF16),
            pltpu.VMEM((128, 12288), BF16),
            pltpu.VMEM((96, 256, 128), BF16),
            pltpu.VMEM((96, 256, 128), BF16),
            *w_scratch,
            pltpu.VMEM((8, 16, 128), jnp.int32),
            pltpu.VMEM((8, 128), jnp.int32),
            pltpu.SMEM((8, 16, 128), jnp.int32),
            pltpu.SMEM((8, 128), jnp.int32),
            pltpu.VMEM((256, 384), BF16),
            pltpu.VMEM((3, 128, 256), BF16),
            pltpu.VMEM((3, 128, 256), BF16),
            *d_scratch,
            pltpu.VMEM((3, 8, 128, 128), BF16),
            pltpu.VMEM((3, 8, 128, 128), BF16),
            pltpu.VMEM((6, 4, 128, 128), BF16),
            pltpu.VMEM((6, 4, 128, 128), BF16),
            pltpu.VMEM((6, 4, 128, 128), BF16),
            pltpu.VMEM((6, 4, 128, 128), BF16),
            pltpu.VMEM((3, 4, 128, 128), BF16),
            pltpu.VMEM((3, 4, 128, 128), BF16),
            pltpu.VMEM((4, 8, 128, 384), F32),
            pltpu.VMEM((4, 8, 128, 384), BF16),
            pltpu.VMEM((4, 8, 128, 384), BF16),
            pltpu.VMEM((3, 8, 128, 384), BF16),
            pltpu.VMEM((7, 128, 384), BF16),
            pltpu.VMEM((128, 384), F32),
            pltpu.VMEM((7, 128, 384), BF16),
            dma((11,)),
            dma((7,)), dma((7,)),
            dma((2,)), dma((2,)),
            dma((3, 2, 2, 2)), dma((3, 2, 2, 2)),
            dma((3, 2)), dma((3, 2)),
            dma((3, 2)), dma((3, 2)),
            dma((3, 2)), dma((3, 2)),
            dma((3, 2, 2, 2)), dma((2, 2, 6)),
            dma((3, 2)), dma((3, 2)),
            dma((4,)), dma((4,)),
            dma((3, 2)), dma((3, 2)),
            dma((7,)), dma((7,)),
        ],
        compiler_params=pltpu.CompilerParams(
            collective_id=0, has_side_effects=True, vmem_limit_bytes=60 * 1024 * 1024),
    )(inputs, out_grads, w1m, w2m, packet)
    return (
        dx,
        jnp.where(live_one, g1, nothing),
        jnp.where(live_two, g2, nothing),
    )


def solution(mesh):
    in_specs = (
        P("seq", None),
        P("seq", None),
        P("mp", "seq", None, None),
        P("mp", "seq"),
        P("mp"),
        P("mp", "seq", None, None),
        P("mp", "seq"),
        P("mp"),
    )
    out_specs = (P("seq", "mp"), P("mp", "seq", None, None), P("mp", "seq", None, None))
    return jax.shard_map(
        per_device, mesh=mesh, in_specs=in_specs, out_specs=out_specs, check_vma=False
    )
```

profile of v0, /device:TPU:1, one launch (start us, length us, event | category | flops | bytes accessed | tf_op | source)
XLA Modules:
  0.0 141.4 jit_solution(8320073659546614741)
XLA Ops:
  0.6 0.7 broadcast_compare_fusion
  1.4 0.8 copy.14
  2.2 0.1 select_reduce_fusion
  2.3 0.8 copy.15
  3.0 0.1 pad_add_fusion.1
  3.1 0.6 pad_add_fusion.pkt_hbm
  3.7 2.1 %broadcast_select_fusion.1.w2_hbm = bf16[6,4,128,128]{3,2,1,0:T(8,128)(2,1)} fusion(bf16[6,4,128,128]{3,2,1,0:T(8,128)(2,1)} %param.13, pred[6,4]{1,0:T(8,128)(4,1)S(1)} %get-tuple-element.9), kind=kLoop, calls=%fused_computation.1 | loop fusion | flops 393216 | bytes 1572888 | tf_op jit(solution)/shard_map/jit(_where)/select_n | solution.py:379
  5.8 2.1 %broadcast_select_fusion.3.w1_hbm = bf16[6,4,128,128]{3,2,1,0:T(8,128)(2,1)} fusion(bf16[6,4,128,128]{3,2,1,0:T(8,128)(2,1)} %param.10, pred[6,4]{1,0:T(8,128)(4,1)S(1)} %get-tuple-element.10), kind=kLoop, calls=%fused_computation.3 | loop fusion | flops 393216 | bytes 1572888 | tf_op jit(solution)/shard_map/jit(_where)/select_n | solution.py:378
  8.0 128.4 %shard_map.103 = (bf16[128,384]{1,0:T(8,128)(2,1)}, bf16[6,4,128,128]{3,2,1,0:T(8,128)(2,1)}, bf16[6,4,128,128]{3,2,1,0:T(8,128)(2,1)}) custom-call(bf16[128,12288]{1,0:T(8,128)(2,1)} %x_hbm.1, bf16[128,12288]{1,0:T(8,128)(2,1)} %dy_hbm.1, bf16[6,4,128,128]{3,2,1,0:T(8,128)(2,1)} %broadcast_select_fusion.3.w1_hbm, ...), custom_call_target="tpu_custom_call" | custom-call | tf_op jit(solution)/shard_map/pallas_call | solution.py:392
  136.4 0.0 copy-start
  136.4 2.2 %broadcast_select_fusion.2 = bf16[6,4,128,128]{3,2,1,0:T(8,128)(2,1)} fusion(bf16[6,4,128,128]{3,2,1,0:T(8,128)(2,1)} %get-tuple-element.7, pred[6,4]{1,0:T(8,128)(4,1)S(1)} %get-tuple-element.10), kind=kLoop, calls=%fused_computation.2 | loop fusion | flops 393216 | bytes 1572888 | tf_op jit(solution)/shard_map/jit(_where)/select_n | solution.py:448
  138.6 2.1 %broadcast_select_fusion = bf16[6,4,128,128]{3,2,1,0:T(8,128)(2,1)} fusion(bf16[6,4,128,128]{3,2,1,0:T(8,128)(2,1)} %get-tuple-element.8, pred[6,4]{1,0:T(8,128)(4,1)S(1)} %get-tuple-element.9), kind=kLoop, calls=%fused_computation | loop fusion | flops 393216 | bytes 1572888 | tf_op jit(solution)/shard_map/jit(_where)/select_n | solution.py:449
  140.7 0.0 copy-done
  140.7 0.6 copy.18
  (1 shorter events, 0.0 us)
Async XLA Ops:
  136.4 4.3 %copy-start = (bf16[128,384]{1,0:T(8,128)(2,1)S(1)}, bf16[128,384]{1,0:T(8,128)(2,1)}, u32[]{:S(2)}) copy-start(bf16[128,384]{1,0:T(8,128)(2,1)} %get-tuple-element.16) | copy-start | bytes 294916
where the time goes:
time: 142 us; the launch traced here: 141 us
  Pallas kernels  128 us (90%)
  other arithmetic  10.1 us (7%)
  local copies, waits for them, and re-layouts  2.18 us (2%)
    pallas_call x1, Pallas kernels, per_device(): pl.pallas_call(kernel, out_shape=(jax.ShapeDtypeStruct((128, 384), BF16),...  128 us

commit v1 on v0

--- a/solution.py
+++ b/solution.py
@@ -17,6 +17,7 @@
 NZ = 8
 COLS = 3
 D_ORDER = (2, 1, 3, 0)
+GROUPS = 4
 
 
 def gelu_both(h):
@@ -28,16 +29,16 @@
 
 
 def kernel(
-    x_hbm, dy_hbm, w1_hbm, w2_hbm, pkt_hbm,
+    x_hbm, dy_hbm, w1_hbm, w2_hbm, rows_sm, count1_sm, cols_sm, count2_sm,
     dx_out, g1_out, g2_out,
     stx, sty, xf, dyf, w1a, w1b, w1c, w2a, w2b, w2c,
-    idxv, invv, idx_sm, inv_sm,
+    pktv, idxv, invv, idx_sm, inv_sm,
     ghcat, ght, actt,
     d1a, d1b, d1c, d2a, d2b, d2c,
     r1, r2, rl1, rl2, rr1, rr2, rp1, rp2,
-    dxo, pxs, prx, yrc, zs, zown, zrc,
-    loc_sem, pk_s, pk_r, xs_s, xs_r, wd_s, wd_r, wp_s, wp_r, wf_s, wf_r,
-    s1_s, s1_r, s2_s, s2_r, sp_s, sp_r, px_s, px_r, y_s, y_r, z_s, z_r,
+    dxo, pxs, prx, y1b, yrc, zs, zown, zrc,
+    hello, loc_sem, pk_s, pk_r, xs_s, xs_r, wd_s, wd_r, wp_s, wp_r, wf_s, wf_r,
+    s1_s, s1_r, s2_s, s2_r, sp_s, sp_r, px_s, px_r, y1_s, y1_r, y_s, y_r, z_s, z_r,
 ):
     w1 = (w1a, w1b, w1c)
     w2 = (w2a, w2b, w2c)
@@ -72,7 +73,6 @@
     local = [
         pltpu.make_async_copy(x_hbm, stx, loc_sem.at[0]),
         pltpu.make_async_copy(dy_hbm, sty, loc_sem.at[1]),
-        pltpu.make_async_copy(pkt_hbm, idxv.at[s], loc_sem.at[2]),
     ]
     wlocal = []
     for j in range(COLS):
@@ -90,19 +90,40 @@
         for cp in pair:
             cp.start()
 
+    def at_z(e):
+        return (s, y * NZ + (z + e) % NZ)
+
     barrier = pltpu.get_barrier_semaphore()
     for e in range(1, 8):
         pl.semaphore_signal(barrier, inc=1, device_id=((s + e) % 8, m), device_id_type=MESH)
     for e in range(1, NY):
         pl.semaphore_signal(
             barrier, inc=1, device_id=(s, ((y + e) % NY) * NZ + z), device_id_type=MESH)
-    for e in range(1, NZ):
-        pl.semaphore_signal(
-            barrier, inc=1, device_id=(s, y * NZ + (z + e) % NZ), device_id_type=MESH)
-    pl.semaphore_wait(barrier, 7 + NY - 1 + NZ - 1)
+    for e in (1, NZ - 1):
+        pl.semaphore_signal(barrier, inc=1, device_id=at_z(e), device_id_type=MESH)
+
+    sub = lax.broadcasted_iota(jnp.int32, (8, 128), 0)
+    lane = lax.broadcasted_iota(jnp.int32, (8, 128), 1)
+    named = jnp.zeros((8, 128), jnp.int32)
+    slot_of = jnp.zeros((8, 128), jnp.int32)
+    for col in range(6):
+        for k in range(4):
+            slot = 4 * s + k
+            row = jnp.where(slot < count1_sm[col], rows_sm[k, col], 96)
+            other = jnp.where(slot < count2_sm[col], cols_sm[k, col], 96)
+            named = jnp.where((sub == col) & (lane == k), row, named)
+            named = jnp.where((sub == col) & (lane == 4 + k), other, named)
+            slot_of = jnp.where((sub == col) & (lane == row), slot + 1, slot_of)
+    pktv[0:8] = named
+    pktv[8:16] = slot_of
+
+    pl.semaphore_wait(barrier, 7 + NY - 1 + 2)
 
     for e in range(1, 8):
-        send(pkt_hbm, idxv.at[s], pk_s.at[e - 1], pk_r.at[e - 1], ((s + e) % 8, m))
+        send(pktv, idxv.at[s], pk_s.at[e - 1], pk_r.at[e - 1], ((s + e) % 8, m))
+    idxv[s] = pktv[...]
+    for e in (1, NZ - 1):
+        pl.semaphore_signal(hello.at[0], inc=1, device_id=at_z(e), device_id_type=MESH)
 
     def direct(j):
         for w, (src, dst) in enumerate(((w1_hbm, w1[j]), (w2_hbm, w2[j]))):
@@ -142,6 +163,9 @@
             arrived((w1, w2)[w][j].at[pl.ds(8 * xo, 8)], wf_s.at[j, w], wf_r.at[j, w])
 
     direct(0)
+    direct(1)
+    direct(2)
+
     for at, (flat, full) in enumerate(((stx, xf), (sty, dyf))):
         local[at].wait()
 
@@ -150,14 +174,17 @@
             return carry
 
         lax.fori_loop(0, 96, regroup, 0)
-        send(full.at[:, pl.ds(0, 128)], full.at[:, pl.ds(128, 128)],
+        send(full.at[pl.ds(0, 96), pl.ds(0, 128)], full.at[pl.ds(0, 96), pl.ds(128, 128)],
              xs_s.at[at], xs_r.at[at], (x * 2 + o, m))
-    direct(1)
+        full[96] = jnp.zeros((256, 128), BF16)
 
     for j in range(COLS):
         w1[j][32] = jnp.zeros((128, 128), BF16)
 
-    local[2].wait()
+    pl.semaphore_wait(hello.at[0], 2)
+    for e in (2, NZ - 2):
+        pl.semaphore_signal(hello.at[1], inc=1, device_id=at_z(e), device_id_type=MESH)
+
     for e in range(1, 8):
         arrived(idxv.at[(s + 8 - e) % 8], pk_s.at[e - 1], pk_r.at[e - 1])
     total = idxv[0, 8:16]
@@ -270,63 +297,86 @@
 
             lax.fori_loop(0, 4, body, 0)
 
-    def input_chunk(d):
-        yy = (y + d) % NY
-
-        def body(q, carry):
-            zz = (z + q + 1) % NZ
-            base = (yy * NZ + zz) * 3
-            rows = []
-            for t in range(3):
-                rows.append(
-                    jnp.concatenate(
-                        [w1[j][inv_sm[3 * c + j, base + t]] for j in range(COLS)], axis=1))
-            rhs = jnp.concatenate(rows, axis=0)
-            out = lax.dot_general(ghcat[...], rhs, NT, preferred_element_type=F32)
-            dxo[d, q] = out[:128]
-            pxs[d, q] = out[128:].astype(BF16)
-            return carry
-
-        lax.fori_loop(0, NZ, body, 0)
-        send(pxs.at[d], prx.at[d], px_s.at[d], px_r.at[d], (x * 2 + o, m))
-
-    def input_pair(d):
-        arrived(prx.at[d], px_s.at[d], px_r.at[d])
-
-        def body(q, carry):
-            both = dxo[d, q] + prx[d, q].astype(F32)
-            if d:
-                prx[d, q] = both.astype(BF16)
-            else:
-                dxo[d, q] = both
-            return carry
-
-        if d:
-            for half in range(2):
-                lax.fori_loop(4 * half, 4 * half + 4, body, 0)
-                send(prx.at[d, pl.ds(4 * half, 4)], yrc.at[d - 1, pl.ds(4 * half, 4)],
-                     y_s.at[d - 1, half], y_r.at[d - 1, half], (s, ((y + d) % NY) * NZ + z))
-        else:
-            lax.fori_loop(0, NZ, body, 0)
-
-    def input_sum(half):
-        for d in range(1, NY):
-            arrived(yrc.at[d - 1, pl.ds(4 * half, 4)], y_s.at[d - 1, half], y_r.at[d - 1, half])
-        for q in range(4 * half, 4 * half + 4):
-            both = dxo[0, q]
-            for d in range(1, NY):
-                both = both + yrc[d - 1, q].astype(F32)
+    def group(ref, d, g):
+        return ref.at[d, pl.ds(2 * g, 2)]
+
+    def input_group(g):
+        for d in D_ORDER:
+            yy = (y + d) % NY
+
+            def body(q, carry):
+                zz = (z + q + 1) % NZ
+                base = (yy * NZ + zz) * 3
+                rows = []
+                for t in range(3):
+                    rows.append(
+                        jnp.concatenate(
+                            [w1[j][inv_sm[3 * c + j, base + t]] for j in range(COLS)], axis=1))
+                rhs = jnp.concatenate(rows, axis=0)
+                out = lax.dot_general(ghcat[...], rhs, NT, preferred_element_type=F32)
+                dxo[d, q] = out[:128]
+                pxs[d, q] = out[128:].astype(BF16)
+                return carry
+
+            lax.fori_loop(2 * g, 2 * g + 2, body, 0)
+            send(group(pxs, d, g), group(prx, d, g), px_s.at[d, g], px_r.at[d, g], (x * 2 + o, m))
+
+    def to_y(d, g):
+        send(group(prx, d, g), yrc.at[d // 2, pl.ds(2 * g, 2)],
+             y_s.at[d // 2, g], y_r.at[d // 2, g], (s, ((y + d) % NY) * NZ + z))
+
+    def input_pair(g):
+        step = 1 if g % 2 == 0 else 3
+        for d in D_ORDER:
+            arrived(group(prx, d, g), px_s.at[d, g], px_r.at[d, g])
+            sent = d in (2, 4 - step)
+
+            def body(q, carry):
+                both = dxo[d, q] + prx[d, q].astype(F32)
+                if sent:
+                    prx[d, q] = both.astype(BF16)
+                else:
+                    dxo[d, q] = both
+                return carry
+
+            lax.fori_loop(2 * g, 2 * g + 2, body, 0)
+            if d == 2:
+                send(group(prx, 2, g), y1b.at[g], y1_s.at[g], y1_r.at[g],
+                     (s, ((y + step) % NY) * NZ + z))
+            elif sent:
+                to_y(d, g)
+
+    def input_added(g):
+        d = 1 if g % 2 == 0 else 3
+        arrived(y1b.at[g], y1_s.at[g], y1_r.at[g])
+        for i in range(2):
+            q = 2 * g + i
+            prx[d, q] = (dxo[d, q] + y1b[g, i].astype(F32)).astype(BF16)
+        to_y(d, g)
+
+    def input_sum(g):
+        for i in range(2):
+            arrived(yrc.at[i, pl.ds(2 * g, 2)], y_s.at[i, g], y_r.at[i, g])
+        for q in (2 * g, 2 * g + 1):
+            both = dxo[0, q] + yrc[0, q].astype(F32) + yrc[1, q].astype(F32)
             if q < NZ - 1:
                 zs[q] = both.astype(BF16)
-                send(zs.at[q], zrc.at[q], z_s.at[q], z_r.at[q], (s, y * NZ + (z + q + 1) % NZ))
+                send(zs.at[q], zrc.at[q], z_s.at[q], z_r.at[q], at_z(q + 1))
             else:
                 zown[...] = both
 
+    def input_last():
+        whole = zown[...]
+        for q in range(NZ - 1):
+            arrived(zrc.at[q], z_s.at[q], z_r.at[q])
+            whole = whole + zrc[q].astype(F32)
+        dx_out[...] = whole.astype(BF16)
+
     forward(0)
-    direct(2)
     forward(1)
-    arrived(xf.at[:, pl.ds(128, 128)], xs_s.at[0], xs_r.at[0])
-    arrived(dyf.at[:, pl.ds(128, 128)], xs_s.at[1], xs_r.at[1])
+    arrived(xf.at[pl.ds(0, 96), pl.ds(128, 128)], xs_s.at[0], xs_r.at[0])
+    arrived(dyf.at[pl.ds(0, 96), pl.ds(128, 128)], xs_s.at[1], xs_r.at[1])
+    pl.semaphore_wait(hello.at[1], 2)
     complete(0)
     forward_pass(0)
     forward(2)
@@ -337,73 +387,74 @@
     complete(2)
     stage_one(0)
     stage_one(1)
-    forward_pass(2)
-    input_chunk(D_ORDER[0])
-    input_chunk(D_ORDER[1])
-    input_pair(D_ORDER[0])
-    input_chunk(D_ORDER[2])
-    input_pair(D_ORDER[1])
-    input_chunk(D_ORDER[3])
-    input_pair(D_ORDER[2])
     stage_two_plain(0)
     stage_two_plain(1)
+    forward_pass(2)
+    input_group(0)
+    input_group(1)
+    input_pair(0)
+    input_group(2)
+    input_pair(1)
+    stage_two_added(0)
+    input_group(3)
+    input_added(0)
+    input_pair(2)
+    input_added(1)
+    stage_two_added(1)
+    input_pair(3)
     weight_grads(2)
     stage_one(2)
     stage_two_plain(2)
-    input_pair(D_ORDER[3])
-    stage_two_added(0)
-    stage_two_added(1)
+    input_sum(0)
+    input_added(2)
+    input_sum(1)
+    input_added(3)
     stage_two_added(2)
-    input_sum(0)
-    input_sum(1)
+    input_sum(2)
+    input_sum(3)
     finish(0)
     finish(1)
-    for q in range(NZ - 1):
-        arrived(zrc.at[q], z_s.at[q], z_r.at[q])
-    whole = zown[...]
-    for q in range(NZ - 1):
-        whole = whole + zrc[q].astype(F32)
-    dx_out[...] = whole.astype(BF16)
+    input_last()
     finish(2)
     for cp in pending:
         cp.wait_send()
 
 
+def copy_out(dx, g1, g2, dx_out, g1_out, g2_out, sem):
+    copies = [pltpu.make_async_copy(dx, dx_out, sem.at[12])]
+    for col in range(6):
+        copies.append(pltpu.make_async_copy(g1.at[col], g1_out.at[col], sem.at[2 * col]))
+        copies.append(pltpu.make_async_copy(g2.at[col], g2_out.at[col], sem.at[2 * col + 1]))
+    for cp in copies:
+        cp.start()
+    for cp in copies:
+        cp.wait()
+
+
 def per_device(inputs, out_grads, w1_blocks, w1_rows, w1_count, w2_blocks, w2_cols, w2_count):
-    s = lax.axis_index("seq")
-    own_ids = s * 4 + jnp.arange(4, dtype=jnp.int32)
-    live_one = (own_ids[None, :] < w1_count[:, None])[:, :, None, None]
-    live_two = (own_ids[None, :] < w2_count[:, None])[:, :, None, None]
-    nothing = jnp.zeros((), BF16)
-    w1m = jnp.where(live_one, w1_blocks, nothing)
-    w2m = jnp.where(live_two, w2_blocks, nothing)
-    lanes = jnp.arange(128, dtype=jnp.int32)
-    slot_of = jnp.sum(
-        jnp.where(w1_rows[:, :, None] == lanes[None, None, :], own_ids[None, :, None] + 1, 0), axis=1)
-    named = jnp.concatenate([w1_rows, w2_cols], axis=1)
-    packet = jnp.concatenate(
-        [jnp.pad(named, ((0, 2), (0, 120))), jnp.pad(slot_of, ((0, 2), (0, 0)))], axis=0)
-
     any_space = pl.BlockSpec(memory_space=pl.ANY)
     vmem = pl.BlockSpec(memory_space=pltpu.VMEM)
+    smem = pl.BlockSpec(memory_space=pltpu.SMEM)
     dma = pltpu.SemaphoreType.DMA
     w_scratch = [pltpu.VMEM((33, 128, 128), BF16)] * 3 + [pltpu.VMEM((32, 128, 128), BF16)] * 3
     d_scratch = [pltpu.VMEM((32, 128, 128), BF16)] * 6
-    dx, g1, g2 = pl.pallas_call(
+    shapes = (
+        jax.ShapeDtypeStruct((128, 384), BF16),
+        jax.ShapeDtypeStruct((6, 4, 128, 128), BF16),
+        jax.ShapeDtypeStruct((6, 4, 128, 128), BF16),
+    )
+    grads = pl.pallas_call(
         kernel,
-        out_shape=(
-            jax.ShapeDtypeStruct((128, 384), BF16),
-            jax.ShapeDtypeStruct((6, 4, 128, 128), BF16),
-            jax.ShapeDtypeStruct((6, 4, 128, 128), BF16),
-        ),
-        in_specs=[any_space] * 5,
+        out_shape=shapes,
+        in_specs=[any_space] * 4 + [smem] * 4,
         out_specs=(vmem, vmem, vmem),
         scratch_shapes=[
             pltpu.VMEM((128, 12288), BF16),
             pltpu.VMEM((128, 12288), BF16),
-            pltpu.VMEM((96, 256, 128), BF16),
-            pltpu.VMEM((96, 256, 128), BF16),
+            pltpu.VMEM((97, 256, 128), BF16),
+            pltpu.VMEM((97, 256, 128), BF16),
             *w_scratch,
+            pltpu.VMEM((16, 128), jnp.int32),
             pltpu.VMEM((8, 16, 128), jnp.int32),
             pltpu.VMEM((8, 128), jnp.int32),
             pltpu.SMEM((8, 16, 128), jnp.int32),
@@ -423,10 +474,12 @@
             pltpu.VMEM((4, 8, 128, 384), F32),
             pltpu.VMEM((4, 8, 128, 384), BF16),
             pltpu.VMEM((4, 8, 128, 384), BF16),
-            pltpu.VMEM((3, 8, 128, 384), BF16),
+            pltpu.VMEM((4, 2, 128, 384), BF16),
+            pltpu.VMEM((2, 8, 128, 384), BF16),
             pltpu.VMEM((7, 128, 384), BF16),
             pltpu.VMEM((128, 384), F32),
             pltpu.VMEM((7, 128, 384), BF16),
+            pltpu.SemaphoreType.REGULAR((2,)),
             dma((11,)),
             dma((7,)), dma((7,)),
             dma((2,)), dma((2,)),
@@ -436,18 +489,21 @@
             dma((3, 2)), dma((3, 2)),
             dma((3, 2, 2, 2)), dma((2, 2, 6)),
             dma((3, 2)), dma((3, 2)),
+            dma((4, 4)), dma((4, 4)),
             dma((4,)), dma((4,)),
-            dma((3, 2)), dma((3, 2)),
+            dma((2, 4)), dma((2, 4)),
             dma((7,)), dma((7,)),
         ],
         compiler_params=pltpu.CompilerParams(
             collective_id=0, has_side_effects=True, vmem_limit_bytes=60 * 1024 * 1024),
-    )(inputs, out_grads, w1m, w2m, packet)
-    return (
-        dx,
-        jnp.where(live_one, g1, nothing),
-        jnp.where(live_two, g2, nothing),
-    )
+    )(inputs, out_grads, w1_blocks, w2_blocks, w1_rows.T, w1_count, w2_cols.T, w2_count)
+    return pl.pallas_call(
+        copy_out,
+        out_shape=shapes,
+        in_specs=[any_space] * 3,
+        out_specs=(any_space,) * 3,
+        scratch_shapes=[dma((13,))],
+    )(*grads)
 
 
 def solution(mesh):

time: 142 us -> 174 us (1.23)
  the two profiles are of different devices: /device:TPU:1 before, /device:TPU:64 now
where the time goes in v1:
time: 174 us; the launch traced here: 172 us
  Pallas kernels  171 us (98%)
    pallas_call x1, Pallas kernels, per_device(): pl.pallas_call(kernel, out_shape=shapes, in_specs=[any_space] * 4 + [smem...  120 us
    pallas_call x1, Pallas kernels, per_device(): pl.pallas_call(copy_out, out_shape=shapes, in_specs=[any_space] * 3, out_...  51.8 us

profile of v1, /device:TPU:64, one launch (start us, length us, event | category | flops | bytes accessed | tf_op | source)
XLA Modules:
  0.0 172.0 jit_solution(2861710092787152781)
XLA Ops:
  0.6 119.5 %shard_map.103 = (bf16[128,384]{1,0:T(8,128)(2,1)}, bf16[6,4,128,128]{3,2,1,0:T(8,128)(2,1)}, bf16[6,4,128,128]{3,2,1,0:T(8,128)(2,1)}) custom-call(bf16[128,12288]{1,0:T(8,128)(2,1)} %x_hbm.1, bf16[128,12288]{1,0:T(8,128)(2,1)} %dy_hbm.1, bf16[6,4,128,128]{3,2,1,0:T(8,128)(2,1)} %w1_hbm.1, bf16[6,4,128,128]{3,2,1,0:T(8,128)(2,1)} %w2_hbm.1, ...), custom_call_target="tpu_custom_call" | custom-call | tf_op jit(solution)/shard_map/pallas_call | solution.py:446
  120.2 51.8 %shard_map.104 = (bf16[128,384]{1,0:T(8,128)(2,1)}, bf16[6,4,128,128]{3,2,1,0:T(8,128)(2,1)}, bf16[6,4,128,128]{3,2,1,0:T(8,128)(2,1)}) custom-call(bf16[128,384]{1,0:T(8,128)(2,1)} %get-tuple-element.6.dx, bf16[6,4,128,128]{3,2,1,0:T(8,128)(2,1)} %get-tuple-element.7.g1, bf16[6,4,128,128]{3,2,1,0:T(8,128)(2,1)} %get-tuple-element.8.g2), custom_call_target="tpu_custom_call" | custom-call | tf_op jit(solution)/shard_map/pallas_call | solution.py:500

commit v2 on v1

--- a/solution.py
+++ b/solution.py
@@ -500,7 +500,7 @@
     return pl.pallas_call(
         copy_out,
         out_shape=shapes,
-        in_specs=[any_space] * 3,
+        in_specs=[vmem] * 3,
         out_specs=(any_space,) * 3,
         scratch_shapes=[dma((13,))],
     )(*grads)

time: 174 us -> 124 us (0.71)
  Pallas kernels: 171 us -> 122 us
    pallas_call x1, Pallas kernels: 51.8 us -> 2.67 us  [per_device(): pl.pallas_call(copy_out, out_shape=shapes, in_specs=[vmem] * 3, out_specs...]
where the time goes in v2:
time: 124 us; the launch traced here: 123 us
  Pallas kernels  122 us (98%)
    pallas_call x1, Pallas kernels, per_device(): pl.pallas_call(kernel, out_shape=shapes, in_specs=[any_space] * 4 + [smem...  120 us
    pallas_call x1, Pallas kernels, per_device(): pl.pallas_call(copy_out, out_shape=shapes, in_specs=[vmem] * 3, out_specs...  2.67 us

profile of v2, /device:TPU:64, one launch (start us, length us, event | category | flops | bytes accessed | tf_op | source)
XLA Modules:
  0.0 122.8 jit_solution(16575989781554694427)
XLA Ops:
  0.6 119.5 %shard_map.103 = (bf16[128,384]{1,0:T(8,128)(2,1)}, bf16[6,4,128,128]{3,2,1,0:T(8,128)(2,1)}, bf16[6,4,128,128]{3,2,1,0:T(8,128)(2,1)}) custom-call(bf16[128,12288]{1,0:T(8,128)(2,1)} %x_hbm.1, bf16[128,12288]{1,0:T(8,128)(2,1)} %dy_hbm.1, bf16[6,4,128,128]{3,2,1,0:T(8,128)(2,1)} %w1_hbm.1, bf16[6,4,128,128]{3,2,1,0:T(8,128)(2,1)} %w2_hbm.1, ...), custom_call_target="tpu_custom_call" | custom-call | tf_op jit(solution)/shard_map/pallas_call | solution.py:446
  120.2 2.7 %shard_map.104 = (bf16[128,384]{1,0:T(8,128)(2,1)}, bf16[6,4,128,128]{3,2,1,0:T(8,128)(2,1)}, bf16[6,4,128,128]{3,2,1,0:T(8,128)(2,1)}) custom-call(bf16[128,384]{1,0:T(8,128)(2,1)} %get-tuple-element.6.dx, bf16[6,4,128,128]{3,2,1,0:T(8,128)(2,1)} %get-tuple-element.7.g1, bf16[6,4,128,128]{3,2,1,0:T(8,128)(2,1)} %get-tuple-element.8.g2), custom_call_target="tpu_custom_call" | custom-call | tf_op jit(solution)/shard_map/pallas_call | solution.py:500

commit v3 on v2

v3 whole, which is shorter than its diff:
```python
import jax
import jax.numpy as jnp
from jax import lax
from jax.experimental import pallas as pl
from jax.experimental.pallas import tpu as pltpu
from jax.sharding import PartitionSpec as P

GELU_C = 0.7978845608028654
CUBIC = 0.044715
BF16 = jnp.bfloat16
F32 = jnp.float32
MESH = pl.DeviceIdType.MESH
NT = (((1,), (1,)), ((), ()))

NX = 4
NY = 4
NZ = 8
COLS = 3
D_ORDER = (2, 1, 3, 0)
PULLS = ((True, 0), (False, 0), (True, 1), (False, 1), (False, 2), (False, 3))


def gelu_both(h):
    arg = GELU_C * (h + CUBIC * h * h * h)
    t = jnp.tanh(arg)
    value = 0.5 * h * (1.0 + t)
    slope = 0.5 * (1.0 + t) + 0.5 * h * (1.0 - t * t) * GELU_C * (1.0 + 3.0 * CUBIC * h * h)
    return value, slope


def kernel(
    x_hbm, dy_hbm, w1_hbm, w2_hbm, rows_sm, count1_sm, cols_sm, count2_sm,
    dx_out, g1_out, g2_out,
    stx, sty, xf, dyf, dyp, w1a, w1b, w1c, w2a, w2b, w2c,
    pktv, idxv, tabv, tab_sm,
    hid, ag_own, ag_sent, ag_got, ghcat, ght, actt, actp,
    d1a, d1b, d1c, d2a, d2b, d2c,
    r1, rl1, rr1, rn2, rp1, rp2,
    dxo, pxs, prx, y1b, yrc, zs, zown, zrc,
    hello, loc_sem, pk_s, pk_r, xs_s, xs_r, wd_s, wd_r, wn_s, wn_r, wp_s, wp_r, wf_s, wf_r,
    pull_s, pull_r, ysh_s, ysh_r, zsh_s, zsh_r, rel_s, rel_r, ag_s, ag_r, ac_s, ac_r,
    s1_s, s1_r, s2_s, s2_r, sn_s, sn_r, sp_s, sp_r, px_s, px_r, y1_s, y1_r, y_s, y_r, z_s, z_r,
):
    w1 = (w1a, w1b, w1c)
    w2 = (w2a, w2b, w2c)
    d1 = (d1a, d1b, d1c)
    d2 = (d2a, d2b, d2c)
    s = lax.axis_index("seq")
    m = lax.axis_index("mp")
    x = s // 2
    c = s % 2
    o = 1 - c
    xl = (x + 3) % 4
    xr = (x + 1) % 4
    xo = (x + 2) % 4
    xp = x + 1 - 2 * (x % 2)
    xn = 3 - x
    y = m // NZ
    z = m % NZ
    zq = z % 4
    way_p = x % 2
    way_n = 1 - way_p
    pending = []

    def send(src, dst, ssem, rsem, dev):
        cp = pltpu.make_async_remote_copy(
            src_ref=src, dst_ref=dst, send_sem=ssem, recv_sem=rsem,
            device_id=dev, device_id_type=MESH,
        )
        cp.start()
        pending.append(cp)

    def arrived(ref, ssem, rsem):
        pltpu.make_async_remote_copy(
            src_ref=ref, dst_ref=ref, send_sem=ssem, recv_sem=rsem,
            device_id=(s, m), device_id_type=MESH,
        ).wait_recv()

    local = [
        pltpu.make_async_copy(x_hbm, stx, loc_sem.at[0]),
        pltpu.make_async_copy(dy_hbm, sty, loc_sem.at[1]),
    ]
    wlocal = []
    for j in range(COLS):
        wlocal.append(
            (
                pltpu.make_async_copy(
                    w1_hbm.at[3 * c + j], w1[j].at[pl.ds(4 * s, 4)], loc_sem.at[3 + 2 * j]),
                pltpu.make_async_copy(
                    w2_hbm.at[3 * c + j], w2[j].at[pl.ds(4 * c, 4)], loc_sem.at[4 + 2 * j]),
            )
        )
    for cp in local:
        cp.start()
    for pair in wlocal:
        for cp in pair:
            cp.start()

    def at_z(e):
        return (s, y * NZ + (z + e) % NZ)

    barrier = pltpu.get_barrier_semaphore()
    for e in range(1, 8):
        pl.semaphore_signal(barrier, inc=1, device_id=((s + e) % 8, m), device_id_type=MESH)
    for e in range(1, NY):
        pl.semaphore_signal(
            barrier, inc=1, device_id=(s, ((y + e) % NY) * NZ + z), device_id_type=MESH)
    for e in (1, NZ - 1):
        pl.semaphore_signal(barrier, inc=1, device_id=at_z(e), device_id_type=MESH)

    sub = lax.broadcasted_iota(jnp.int32, (8, 128), 0)
    lane = lax.broadcasted_iota(jnp.int32, (8, 128), 1)
    named = jnp.zeros((8, 128), jnp.int32)
    slot_of = jnp.zeros((8, 128), jnp.int32)
    for col in range(6):
        for k in range(4):
            slot = 4 * s + k
            row = jnp.where(slot < count1_sm[col], rows_sm[k, col], 96)
            other = jnp.where(slot < count2_sm[col], cols_sm[k, col], 96)
            named = jnp.where((sub == col) & (lane == 8 * s + k), row, named)
            named = jnp.where((sub == col) & (lane == 8 * s + 4 + k), other, named)
            slot_of = jnp.where((sub == col) & (lane == row), slot + 1, slot_of)
    pktv[0:8] = named
    pktv[8:16] = slot_of

    def regrouped(at, flat, full):
        local[at].wait()

        def body(r, carry):
            full[r, 0:128] = flat[:, pl.ds(pl.multiple_of(r * 128, 128), 128)]
            return carry

        lax.fori_loop(0, 96, body, 0, unroll=8)
        full[96] = jnp.zeros((256, 128), BF16)

    pl.semaphore_wait(barrier, 7 + NY - 1 + 2)

    pulls = []

    def pull():
        n = len(pulls)
        along_z, i = PULLS[n]
        first = 64 + 8 * zq + 4 * i if along_z else 16 * y + 4 * i
        send(dyf.at[pl.ds(first, 4), pl.ds(0, 128)], dyp.at[pl.ds(first, 4), pl.ds(0, 128)],
             pull_s.at[n], pull_r.at[n], (xp * 2 + c, m))
        pulls.append(pending.pop())

    def next_pull():
        pulls[len(pulls) - 2].wait_send()
        pull()

    for e in range(1, 8):
        send(pktv, idxv.at[s], pk_s.at[e - 1], pk_r.at[e - 1], ((s + e) % 8, m))
    idxv[s] = pktv[...]
    for e in (1, NZ - 1):
        pl.semaphore_signal(hello.at[0], inc=1, device_id=at_z(e), device_id_type=MESH)

    def direct_one(j, xd, way):
        for cd in range(2):
            send(w1_hbm.at[3 * cd + j], w1[j].at[pl.ds(4 * s, 4)],
                 wd_s.at[j, way, cd], wd_r.at[j, way, c], (xd * 2 + cd, m))

    def core_one(j):
        send(w1_hbm.at[3 * o + j], w1[j].at[pl.ds(4 * s, 4)],
             wp_s.at[j, 0], wp_r.at[j, 0], (x * 2 + o, m))

    def direct_two(j):
        for cd in range(2):
            send(w2_hbm.at[3 * cd + j], w2[j].at[pl.ds(8 + 4 * c, 4)],
                 wn_s.at[j, cd], wn_r.at[j, c], (xn * 2 + cd, m))
        send(w2_hbm.at[3 * o + j], w2[j].at[pl.ds(4 * c, 4)],
             wp_s.at[j, 1], wp_r.at[j, 1], (x * 2 + o, m))

    def from_chip(j, xs, way, cs):
        arrived(w1[j].at[pl.ds(8 * xs + 4 * cs, 4)], wd_s.at[j, way, cs], wd_r.at[j, way, cs])

    def forward(j, xs, xd, way):
        from_chip(j, xs, way, way)
        part = w1[j].at[pl.ds(8 * xs + 4 * way, 4)]
        send(part, part, wf_s.at[j, way], wf_r.at[j, way], (xd * 2 + c, m))

    def complete_one(j):
        wlocal[j][0].wait()
        arrived(w1[j].at[pl.ds(8 * x + 4 * o, 4)], wp_s.at[j, 0], wp_r.at[j, 0])
        from_chip(j, xn, way_p, 1 - way_p)
        from_chip(j, xp, way_n, 1 - way_n)
        for way in range(2):
            arrived(w1[j].at[pl.ds(8 * xo + 4 * way, 4)], wf_s.at[j, way], wf_r.at[j, way])

    def complete_two(j):
        wlocal[j][1].wait()
        arrived(w2[j].at[pl.ds(4 * o, 4)], wp_s.at[j, 1], wp_r.at[j, 1])
        for cs in range(2):
            arrived(w2[j].at[pl.ds(8 + 4 * cs, 4)], wn_s.at[j, cs], wn_r.at[j, cs])

    for j in range(COLS):
        direct_one(j, xn, way_n)

    def to_core(at, full):
        send(full.at[pl.ds(0, 96), pl.ds(0, 128)], full.at[pl.ds(0, 96), pl.ds(128, 128)],
             xs_s.at[at], xs_r.at[at], (x * 2 + o, m))

    regrouped(1, sty, dyf)
    pull()
    pull()
    for j in range(COLS):
        core_one(j)
    regrouped(0, stx, xf)
    to_core(1, dyf)
    next_pull()
    dyp[96] = jnp.zeros((256, 128), BF16)

    for j in range(COLS):
        w1[j][32] = jnp.zeros((128, 128), BF16)

    pl.semaphore_wait(hello.at[0], 2)
    for e in (2, NZ - 2):
        pl.semaphore_signal(hello.at[1], inc=1, device_id=at_z(e), device_id_type=MESH)

    def part_of(first, half):
        return dyp.at[pl.ds(first, 4), pl.ds(128 * half, 128)]

    def relay(n, first):
        send(part_of(first, 0), part_of(first, 1), rel_s.at[n], rel_r.at[n], (x * 2 + o, m))

    def y_first(e, i):
        return 16 * ((y + 4 - e) % 4) + 4 * i

    def z_first(e, i):
        return 64 + 8 * ((zq + 4 - e) % 4) + 4 * i

    def share(n):
        along_z, i = PULLS[n]
        first = z_first(0, i) if along_z else y_first(0, i)
        arrived(part_of(first, 0), pull_s.at[n], pull_r.at[n])
        for e in (1, 3, 2):
            if along_z:
                send(part_of(first, 0), part_of(first, 0), zsh_s.at[e - 1, i], zsh_r.at[e - 1, i],
                     (s, y * NZ + z - zq + (zq + e) % 4))
            else:
                send(part_of(first, 0), part_of(first, 0), ysh_s.at[e - 1, i], ysh_r.at[e - 1, i],
                     (s, ((y + e) % NY) * NZ + z))
        relay(n, first)

    def relay_y(i):
        for e in range(1, 4):
            arrived(part_of(y_first(e, i), 0), ysh_s.at[e - 1, i], ysh_r.at[e - 1, i])
            relay(6 + 4 * (e - 1) + i, y_first(e, i))

    def relay_z(i):
        for e in range(1, 4):
            arrived(part_of(z_first(e, i), 0), zsh_s.at[e - 1, i], zsh_r.at[e - 1, i])
            relay(18 + 2 * (e - 1) + i, z_first(e, i))

    def partner_ready():
        for n, (along_z, i) in enumerate(PULLS):
            first = z_first(0, i) if along_z else y_first(0, i)
            arrived(part_of(first, 1), rel_s.at[n], rel_r.at[n])
        for e in range(1, 4):
            for i in range(4):
                n = 6 + 4 * (e - 1) + i
                arrived(part_of(y_first(e, i), 1), rel_s.at[n], rel_r.at[n])
            for i in range(2):
                n = 18 + 2 * (e - 1) + i
                arrived(part_of(z_first(e, i), 1), rel_s.at[n], rel_r.at[n])

    for e in range(1, 8):
        arrived(idxv.at[(s + 8 - e) % 8], pk_s.at[e - 1], pk_r.at[e - 1])
    total = idxv[0]
    for t in range(1, 8):
        total = total + idxv[t]
    tabv[0:8] = total[0:8]
    tabv[8:16] = jnp.where(total[8:16] > 0, total[8:16] - 1, 32)
    to_sm = pltpu.make_async_copy(tabv, tab_sm, loc_sem.at[9])
    to_sm.start()
    to_sm.wait()

    def picked(ref, who, col, first):
        return jnp.concatenate([ref[tab_sm[col, 8 * who + first + u]] for u in range(4)], axis=1)

    def owner(p):
        other = p // 2
        return 2 * (x + other * (xn - x)) + p % 2

    def hidden_pass(j):
        col = 3 * c + j

        def body(p, h):
            xs = picked(xf, p, col, 0)
            ws = w1[j][pl.ds(4 * p, 4)].reshape(512, 128)
            return h + jnp.dot(xs, ws, preferred_element_type=F32)

        hid[j] = lax.fori_loop(0, 8, body, jnp.zeros((256, 128), F32))

    def act_grads(j, full):
        col = 3 * c + j

        def body(p, a):
            vs = jnp.concatenate([w2[j][4 * p + u] for u in range(4)], axis=1)
            ys = picked(full, owner(p), col, 4)
            return a + lax.dot_general(ys, vs, NT, preferred_element_type=F32)

        return lax.fori_loop(0, 4, body, jnp.zeros((256, 128), F32))

    def act_own(j):
        ag_own[j] = act_grads(j, dyf)

    def act_other(j):
        ag_sent[j] = act_grads(j, dyp).astype(BF16)
        send(ag_sent.at[j], ag_got.at[j], ag_s.at[j], ag_r.at[j], (xp * 2 + c, m))

    def activate(j):
        value, slope = gelu_both(hid[j])
        hid[j] = slope
        actt[j] = value.T.astype(BF16)
        send(actt.at[j], actp.at[j], ac_s.at[j], ac_r.at[j], (xp * 2 + c, m))

    def hidden_grads(j):
        arrived(ag_got.at[j], ag_s.at[j], ag_r.at[j])
        grad = (ag_own[j] + ag_got[j].astype(F32)) * hid[j]
        ghcat[:, j * 128:(j + 1) * 128] = grad.astype(BF16)
        ght[j] = grad.T.astype(BF16)

    def grads_one(j):
        col = 3 * c + j

        def body(q, carry):
            who = (2 * xo + q) % 8
            t1 = jnp.dot(ght[j], picked(xf, who, col, 0), preferred_element_type=F32)
            for u in range(4):
                d1[j][4 * who + u] = t1[:, 128 * u:128 * (u + 1)].astype(BF16)
            return carry

        lax.fori_loop(0, 8, body, 0)
        send(d1[j].at[pl.ds(8 * xo, 4)], r1.at[j, pl.ds(0, 4)],
             s1_s.at[j, 0], s1_r.at[j, 0], (xr * 2 + c, m))
        send(d1[j].at[pl.ds(8 * xo + 4, 4)], r1.at[j, pl.ds(4, 4)],
             s1_s.at[j, 1], s1_r.at[j, 1], (xl * 2 + c, m))
        send(d1[j].at[pl.ds(8 * xr + 4, 4)], rl1.at[col],
             s2_s.at[j, 0, 1], s2_r.at[0, col], (xr * 2 + 1, m))
        send(d1[j].at[pl.ds(8 * xl, 4)], rr1.at[col],
             s2_s.at[j, 1, 0], s2_r.at[1, col], (xl * 2, m))
        send(d1[j].at[pl.ds(8 * x + 4 * o, 4)], rp1.at[j], sp_s.at[j, 0], sp_r.at[j, 0], (x * 2 + o, m))

    def grads_two(j):
        col = 3 * c + j
        arrived(actp.at[j], ac_s.at[j], ac_r.at[j])

        def body(p, carry):
            t2 = jnp.dot(actt[j], picked(dyf, owner(p), col, 4), preferred_element_type=F32)
            t2 = t2 + jnp.dot(actp[j], picked(dyp, owner(p), col, 4), preferred_element_type=F32)
            for u in range(4):
                d2[j][4 * p + u] = t2[:, 128 * u:128 * (u + 1)].astype(BF16)
            return carry

        lax.fori_loop(0, 4, body, 0)
        for co in range(2):
            send(d2[j].at[pl.ds(8 + 4 * co, 4)], rn2.at[col],
                 sn_s.at[j, co], sn_r.at[col], (xn * 2 + co, m))
        send(d2[j].at[pl.ds(4 * o, 4)], rp2.at[j], sp_s.at[j, 1], sp_r.at[j, 1], (x * 2 + o, m))

    def grads_added(j):
        col = 3 * c + j
        for way, xd, into in ((0, xr, rl1), (1, xl, rr1)):
            arrived(r1.at[j, pl.ds(4 * way, 4)], s1_s.at[j, way], s1_r.at[j, way])

            def body(k, carry):
                at = 8 * xd + 4 * way + k
                d1[j][at] = (d1[j][at].astype(F32) + r1[j, 4 * way + k].astype(F32)).astype(BF16)
                return carry

            lax.fori_loop(0, 4, body, 0)
            send(d1[j].at[pl.ds(8 * xd + 4 * way, 4)], into.at[col],
                 s2_s.at[j, way, way], s2_r.at[way, col], (xd * 2 + way, m))

    def finish(j):
        for cc, own in ((c, True), (o, False)):
            col = 3 * cc + j
            arrived(rn2.at[col], sn_s.at[j, 0], sn_r.at[col])
            arrived(rl1.at[col], s2_s.at[j, 0, 0], s2_r.at[0, col])
            arrived(rr1.at[col], s2_s.at[j, 1, 0], s2_r.at[1, col])
            if not own:
                arrived(rp1.at[j], sp_s.at[j, 0], sp_r.at[j, 0])
                arrived(rp2.at[j], sp_s.at[j, 1], sp_r.at[j, 1])

            def body(k, carry):
                mine1 = d1[j][4 * s + k] if own else rp1[j, k]
                mine2 = d2[j][4 * c + k] if own else rp2[j, k]
                t1 = mine1.astype(F32) + rl1[col, k].astype(F32) + rr1[col, k].astype(F32)
                t2 = mine2.astype(F32) + rn2[col, k].astype(F32)
                g1_out[col, k] = t1.T.astype(BF16)
                g2_out[col, k] = t2.astype(BF16)
                return carry

            lax.fori_loop(0, 4, body, 0)

    def group(ref, d, g):
        return ref.at[d, pl.ds(2 * g, 2)]

    def input_group(g):
        for d in D_ORDER:
            yy = (y + d) % NY

            def body(q, carry):
                zz = (z + q + 1) % NZ
                base = (yy * NZ + zz) * 3
                rows = []
                for t in range(3):
                    rows.append(
                        jnp.concatenate(
                            [w1[j][tab_sm[8 + 3 * c + j, base + t]] for j in range(COLS)], axis=1))
                rhs = jnp.concatenate(rows, axis=0)
                out = lax.dot_general(ghcat[...], rhs, NT, preferred_element_type=F32)
                dxo[d, q] = out[:128]
                pxs[d, q] = out[128:].astype(BF16)
                return carry

            lax.fori_loop(2 * g, 2 * g + 2, body, 0)
            send(group(pxs, d, g), group(prx, d, g), px_s.at[d, g], px_r.at[d, g], (x * 2 + o, m))

    def to_y(d, g):
        send(group(prx, d, g), yrc.at[d // 2, pl.ds(2 * g, 2)],
             y_s.at[d // 2, g], y_r.at[d // 2, g], (s, ((y + d) % NY) * NZ + z))

    def input_pair(g):
        step = 1 if g % 2 == 0 else 3
        for d in D_ORDER:
            arrived(group(prx, d, g), px_s.at[d, g], px_r.at[d, g])
            sent = d in (2, 4 - step)

            def body(q, carry):
                both = dxo[d, q] + prx[d, q].astype(F32)
                if sent:
                    prx[d, q] = both.astype(BF16)
                else:
                    dxo[d, q] = both
                return carry

            lax.fori_loop(2 * g, 2 * g + 2, body, 0)
            if d == 2:
                send(group(prx, 2, g), y1b.at[g], y1_s.at[g], y1_r.at[g],
                     (s, ((y + step) % NY) * NZ + z))
            elif sent:
                to_y(d, g)

    def input_added(g):
        d = 1 if g % 2 == 0 else 3
        arrived(y1b.at[g], y1_s.at[g], y1_r.at[g])
        for i in range(2):
            q = 2 * g + i
            prx[d, q] = (dxo[d, q] + y1b[g, i].astype(F32)).astype(BF16)
        to_y(d, g)

    def input_sum(g):
        for i in range(2):
            arrived(yrc.at[i, pl.ds(2 * g, 2)], y_s.at[i, g], y_r.at[i, g])
        for q in (2 * g, 2 * g + 1):
            both = dxo[0, q] + yrc[0, q].astype(F32) + yrc[1, q].astype(F32)
            if q < NZ - 1:
                zs[q] = both.astype(BF16)
                send(zs.at[q], zrc.at[q], z_s.at[q], z_r.at[q], at_z(q + 1))
            else:
                zown[...] = both

    def input_last():
        whole = zown[...]
        for q in range(NZ - 1):
            arrived(zrc.at[q], z_s.at[q], z_r.at[q])
            whole = whole + zrc[q].astype(F32)
        dx_out[...] = whole.astype(BF16)

    pl.semaphore_wait(hello.at[1], 2)
    share(0)
    next_pull()
    share(1)
    next_pull()
    share(2)
    next_pull()
    direct_two(0)
    share(3)
    direct_two(1)
    direct_one(0, xp, way_p)
    share(4)
    direct_two(2)
    direct_one(1, xp, way_p)
    share(5)
    direct_one(2, xp, way_p)
    forward(0, xn, xp, way_p)
    forward(1, xn, xp, way_p)
    forward(2, xn, xp, way_p)
    to_core(0, xf)
    relay_z(0)
    relay_y(0)
    forward(0, xp, xn, way_n)
    arrived(dyf.at[pl.ds(0, 96), pl.ds(128, 128)], xs_s.at[1], xs_r.at[1])
    arrived(xf.at[pl.ds(0, 96), pl.ds(128, 128)], xs_s.at[0], xs_r.at[0])
    relay_z(1)
    relay_y(1)
    forward(1, xp, xn, way_n)
    relay_y(2)
    complete_two(0)
    act_own(0)
    relay_y(3)
    forward(2, xp, xn, way_n)
    complete_two(1)
    complete_two(2)
    partner_ready()
    act_other(0)
    act_other(1)
    act_other(2)
    act_own(1)
    act_own(2)
    complete_one(0)
    hidden_pass(0)
    activate(0)
    hidden_grads(0)
    complete_one(1)
    hidden_pass(1)
    activate(1)
    hidden_grads(1)
    grads_one(0)
    complete_one(2)
    hidden_pass(2)
    activate(2)
    hidden_grads(2)
    input_group(0)
    grads_two(0)
    input_group(1)
    input_pair(0)
    grads_one(1)
    input_group(2)
    input_pair(1)
    input_added(0)
    grads_two(1)
    grads_added(0)
    input_group(3)
    input_pair(2)
    input_added(1)
    input_sum(0)
    input_pair(3)
    grads_one(2)
    grads_added(1)
    input_added(2)
    input_sum(1)
    grads_two(2)
    input_added(3)
    grads_added(2)
    input_sum(2)
    finish(0)
    input_sum(3)
    finish(1)
    input_last()
    finish(2)
    for cp in pending + pulls[-2:]:
        cp.wait_send()


def copy_out(dx, g1, g2, dx_out, g1_out, g2_out, sem):
    copies = [pltpu.make_async_copy(dx, dx_out, sem.at[12])]
    for col in range(6):
        copies.append(pltpu.make_async_copy(g1.at[col], g1_out.at[col], sem.at[2 * col]))
        copies.append(pltpu.make_async_copy(g2.at[col], g2_out.at[col], sem.at[2 * col + 1]))
    for cp in copies:
        cp.start()
    for cp in copies:
        cp.wait()


def per_device(inputs, out_grads, w1_blocks, w1_rows, w1_count, w2_blocks, w2_cols, w2_count):
    any_space = pl.BlockSpec(memory_space=pl.ANY)
    vmem = pl.BlockSpec(memory_space=pltpu.VMEM)
    smem = pl.BlockSpec(memory_space=pltpu.SMEM)
    dma = pltpu.SemaphoreType.DMA
    w_scratch = [pltpu.VMEM((33, 128, 128), BF16)] * 3 + [pltpu.VMEM((16, 128, 128), BF16)] * 3
    d_scratch = [pltpu.VMEM((32, 128, 128), BF16)] * 3 + [pltpu.VMEM((16, 128, 128), BF16)] * 3
    shapes = (
        jax.ShapeDtypeStruct((128, 384), BF16),
        jax.ShapeDtypeStruct((6, 4, 128, 128), BF16),
        jax.ShapeDtypeStruct((6, 4, 128, 128), BF16),
    )
    grads = pl.pallas_call(
        kernel,
        out_shape=shapes,
        in_specs=[any_space] * 4 + [smem] * 4,
        out_specs=(vmem, vmem, vmem),
        scratch_shapes=[
            pltpu.VMEM((128, 12288), BF16),
            pltpu.VMEM((128, 12288), BF16),
            pltpu.VMEM((97, 256, 128), BF16),
            pltpu.VMEM((97, 256, 128), BF16),
            pltpu.VMEM((97, 256, 128), BF16),
            *w_scratch,
            pltpu.VMEM((16, 128), jnp.int32),
            pltpu.VMEM((8, 16, 128), jnp.int32),
            pltpu.VMEM((16, 128), jnp.int32),
            pltpu.SMEM((16, 128), jnp.int32),
            *[pltpu.VMEM((3, 256, 128), F32)] * 2,
            *[pltpu.VMEM((3, 256, 128), BF16)] * 2,
            pltpu.VMEM((256, 384), BF16),
            *[pltpu.VMEM((3, 128, 256), BF16)] * 3,
            *d_scratch,
            pltpu.VMEM((3, 8, 128, 128), BF16),
            pltpu.VMEM((6, 4, 128, 128), BF16),
            pltpu.VMEM((6, 4, 128, 128), BF16),
            pltpu.VMEM((6, 4, 128, 128), BF16),
            pltpu.VMEM((3, 4, 128, 128), BF16),
            pltpu.VMEM((3, 4, 128, 128), BF16),
            pltpu.VMEM((4, 8, 128, 384), F32),
            pltpu.VMEM((4, 8, 128, 384), BF16),
            pltpu.VMEM((4, 8, 128, 384), BF16),
            pltpu.VMEM((4, 2, 128, 384), BF16),
            pltpu.VMEM((2, 8, 128, 384), BF16),
            pltpu.VMEM((7, 128, 384), BF16),
            pltpu.VMEM((128, 384), F32),
            pltpu.VMEM((7, 128, 384), BF16),
            pltpu.SemaphoreType.REGULAR((2,)),
            dma((11,)),
            dma((7,)), dma((7,)),
            dma((2,)), dma((2,)),
            dma((3, 2, 2)), dma((3, 2, 2)),
            dma((3, 2)), dma((3, 2)),
            dma((3, 2)), dma((3, 2)),
            dma((3, 2)), dma((3, 2)),
            dma((6,)), dma((6,)),
            dma((3, 4)), dma((3, 4)),
            dma((3, 2)), dma((3, 2)),
            dma((24,)), dma((24,)),
            dma((3,)), dma((3,)),
            dma((3,)), dma((3,)),
            dma((3, 2)), dma((3, 2)),
            dma((3, 2, 2)), dma((2, 6)),
            dma((3, 2)), dma((6,)),
            dma((3, 2)), dma((3, 2)),
            dma((4, 4)), dma((4, 4)),
            dma((4,)), dma((4,)),
            dma((2, 4)), dma((2, 4)),
            dma((7,)), dma((7,)),
        ],
        compiler_params=pltpu.CompilerParams(
            collective_id=0, has_side_effects=True, vmem_limit_bytes=60 * 1024 * 1024),
    )(inputs, out_grads, w1_blocks, w2_blocks, w1_rows.T, w1_count, w2_cols.T, w2_count)
    return pl.pallas_call(
        copy_out,
        out_shape=shapes,
        in_specs=[vmem] * 3,
        out_specs=(any_space,) * 3,
        scratch_shapes=[dma((13,))],
    )(*grads)


def solution(mesh):
    in_specs = (
        P("seq", None),
        P("seq", None),
        P("mp", "seq", None, None),
        P("mp", "seq"),
        P("mp"),
        P("mp", "seq", None, None),
        P("mp", "seq"),
        P("mp"),
    )
    out_specs = (P("seq", "mp"), P("mp", "seq", None, None), P("mp", "seq", None, None))
    return jax.shard_map(
        per_device, mesh=mesh, in_specs=in_specs, out_specs=out_specs, check_vma=False
    )
```

time: 124 us -> 115 us (0.927)
  Pallas kernels: 122 us -> 113 us
    pallas_call x1, Pallas kernels: 120 us -> 111 us  [per_device(): pl.pallas_call(kernel, out_shape=shapes, in_specs=[any_space] * 4 + [smem...]
where the time goes in v3:
time: 115 us; the launch traced here: 114 us
  Pallas kernels  113 us (98%)
    pallas_call x1, Pallas kernels, per_device(): pl.pallas_call(kernel, out_shape=shapes, in_specs=[any_space] * 4 + [smem...  111 us
    pallas_call x1, Pallas kernels, per_device(): pl.pallas_call(copy_out, out_shape=shapes, in_specs=[vmem] * 3, out_specs...  2.67 us

profile of v3, /device:TPU:64, one launch (start us, length us, event | category | flops | bytes accessed | tf_op | source)
XLA Modules:
  0.0 113.9 jit_solution(8866645429741070467)
XLA Ops:
  0.6 110.6 %shard_map.103 = (bf16[128,384]{1,0:T(8,128)(2,1)}, bf16[6,4,128,128]{3,2,1,0:T(8,128)(2,1)}, bf16[6,4,128,128]{3,2,1,0:T(8,128)(2,1)}) custom-call(bf16[128,12288]{1,0:T(8,128)(2,1)} %x_hbm.1, bf16[128,12288]{1,0:T(8,128)(2,1)} %dy_hbm.1, bf16[6,4,128,128]{3,2,1,0:T(8,128)(2,1)} %w1_hbm.1, bf16[6,4,128,128]{3,2,1,0:T(8,128)(2,1)} %w2_hbm.1, ...), custom_call_target="tpu_custom_call" | custom-call | tf_op jit(solution)/shard_map/pallas_call | solution.py:581
  111.3 2.7 %shard_map.104 = (bf16[128,384]{1,0:T(8,128)(2,1)}, bf16[6,4,128,128]{3,2,1,0:T(8,128)(2,1)}, bf16[6,4,128,128]{3,2,1,0:T(8,128)(2,1)}) custom-call(bf16[128,384]{1,0:T(8,128)(2,1)} %get-tuple-element.6.dx, bf16[6,4,128,128]{3,2,1,0:T(8,128)(2,1)} %get-tuple-element.7.g1, bf16[6,4,128,128]{3,2,1,0:T(8,128)(2,1)} %get-tuple-element.8.g2), custom_call_target="tpu_custom_call" | custom-call | tf_op jit(solution)/shard_map/pallas_call | solution.py:642

commit v4 on v3

--- a/solution.py
+++ b/solution.py
@@ -30,14 +30,14 @@
 
 def kernel(
     x_hbm, dy_hbm, w1_hbm, w2_hbm, rows_sm, count1_sm, cols_sm, count2_sm,
-    dx_out, g1_out, g2_out,
+    dx_out, g1_hbm, g2_hbm,
     stx, sty, xf, dyf, dyp, w1a, w1b, w1c, w2a, w2b, w2c,
     pktv, idxv, tabv, tab_sm,
     hid, ag_own, ag_sent, ag_got, ghcat, ght, actt, actp,
     d1a, d1b, d1c, d2a, d2b, d2c,
     r1, rl1, rr1, rn2, rp1, rp2,
-    dxo, pxs, prx, y1b, yrc, zs, zown, zrc,
-    hello, loc_sem, pk_s, pk_r, xs_s, xs_r, wd_s, wd_r, wn_s, wn_r, wp_s, wp_r, wf_s, wf_r,
+    g1_out, g2_out, dxo, pxs, prx, y1b, yrc, zs, zown, zrc,
+    out_sem, hello, loc_sem, pk_s, pk_r, xs_s, xs_r, wd_s, wd_r, wn_s, wn_r, wp_s, wp_r, wf_s, wf_r,
     pull_s, pull_r, ysh_s, ysh_r, zsh_s, zsh_r, rel_s, rel_r, ag_s, ag_r, ac_s, ac_r,
     s1_s, s1_r, s2_s, s2_r, sn_s, sn_r, sp_s, sp_r, px_s, px_r, y1_s, y1_r, y_s, y_r, z_s, z_r,
 ):
@@ -61,6 +61,7 @@
     way_p = x % 2
     way_n = 1 - way_p
     pending = []
+    leaving = []
 
     def send(src, dst, ssem, rsem, dev):
         cp = pltpu.make_async_remote_copy(
@@ -332,14 +333,10 @@
             return carry
 
         lax.fori_loop(0, 8, body, 0)
-        send(d1[j].at[pl.ds(8 * xo, 4)], r1.at[j, pl.ds(0, 4)],
-             s1_s.at[j, 0], s1_r.at[j, 0], (xr * 2 + c, m))
-        send(d1[j].at[pl.ds(8 * xo + 4, 4)], r1.at[j, pl.ds(4, 4)],
-             s1_s.at[j, 1], s1_r.at[j, 1], (xl * 2 + c, m))
-        send(d1[j].at[pl.ds(8 * xr + 4, 4)], rl1.at[col],
-             s2_s.at[j, 0, 1], s2_r.at[0, col], (xr * 2 + 1, m))
-        send(d1[j].at[pl.ds(8 * xl, 4)], rr1.at[col],
-             s2_s.at[j, 1, 0], s2_r.at[1, col], (xl * 2, m))
+        send(d1[j].at[pl.ds(8 * xo, 8)], r1.at[j], s1_s.at[j], s1_r.at[j], (xp * 2 + c, m))
+        for co in range(2):
+            send(d1[j].at[pl.ds(8 * xp + 4 * co, 4)], rr1.at[col],
+                 s2_s.at[j, 1, co], s2_r.at[1, col], (xp * 2 + co, m))
         send(d1[j].at[pl.ds(8 * x + 4 * o, 4)], rp1.at[j], sp_s.at[j, 0], sp_r.at[j, 0], (x * 2 + o, m))
 
     def grads_two(j):
@@ -361,17 +358,17 @@
 
     def grads_added(j):
         col = 3 * c + j
-        for way, xd, into in ((0, xr, rl1), (1, xl, rr1)):
-            arrived(r1.at[j, pl.ds(4 * way, 4)], s1_s.at[j, way], s1_r.at[j, way])
-
-            def body(k, carry):
-                at = 8 * xd + 4 * way + k
-                d1[j][at] = (d1[j][at].astype(F32) + r1[j, 4 * way + k].astype(F32)).astype(BF16)
-                return carry
-
-            lax.fori_loop(0, 4, body, 0)
-            send(d1[j].at[pl.ds(8 * xd + 4 * way, 4)], into.at[col],
-                 s2_s.at[j, way, way], s2_r.at[way, col], (xd * 2 + way, m))
+        arrived(r1.at[j], s1_s.at[j], s1_r.at[j])
+
+        def body(k, carry):
+            at = 8 * xn + k
+            d1[j][at] = (d1[j][at].astype(F32) + r1[j, k].astype(F32)).astype(BF16)
+            return carry
+
+        lax.fori_loop(0, 8, body, 0)
+        for co in range(2):
+            send(d1[j].at[pl.ds(8 * xn + 4 * co, 4)], rl1.at[col],
+                 s2_s.at[j, 0, co], s2_r.at[0, col], (xn * 2 + co, m))
 
     def finish(j):
         for cc, own in ((c, True), (o, False)):
@@ -393,6 +390,10 @@
                 return carry
 
             lax.fori_loop(0, 4, body, 0)
+            for at, (part, whole) in enumerate(((g1_out, g1_hbm), (g2_out, g2_hbm))):
+                cp = pltpu.make_async_copy(part.at[col], whole.at[col], out_sem.at[at, col])
+                cp.start()
+                leaving.append(cp)
 
     def group(ref, d, g):
         return ref.at[d, pl.ds(2 * g, 2)]
@@ -400,22 +401,18 @@
     def input_group(g):
         for d in D_ORDER:
             yy = (y + d) % NY
-
-            def body(q, carry):
-                zz = (z + q + 1) % NZ
-                base = (yy * NZ + zz) * 3
-                rows = []
+            rows = []
+            for q in (2 * g, 2 * g + 1):
+                base = (yy * NZ + (z + q + 1) % NZ) * 3
                 for t in range(3):
                     rows.append(
                         jnp.concatenate(
                             [w1[j][tab_sm[8 + 3 * c + j, base + t]] for j in range(COLS)], axis=1))
-                rhs = jnp.concatenate(rows, axis=0)
-                out = lax.dot_general(ghcat[...], rhs, NT, preferred_element_type=F32)
-                dxo[d, q] = out[:128]
-                pxs[d, q] = out[128:].astype(BF16)
-                return carry
-
-            lax.fori_loop(2 * g, 2 * g + 2, body, 0)
+            rhs = jnp.concatenate(rows, axis=0)
+            out = lax.dot_general(ghcat[...], rhs, NT, preferred_element_type=F32)
+            for i in range(2):
+                dxo[d, 2 * g + i] = out[:128, 384 * i:384 * (i + 1)]
+                pxs[d, 2 * g + i] = out[128:, 384 * i:384 * (i + 1)].astype(BF16)
             send(group(pxs, d, g), group(prx, d, g), px_s.at[d, g], px_r.at[d, g], (x * 2 + o, m))
 
     def to_y(d, g):
@@ -527,22 +524,22 @@
     grads_two(0)
     input_group(1)
     input_pair(0)
+    grads_added(0)
     grads_one(1)
     input_group(2)
     input_pair(1)
     input_added(0)
     grads_two(1)
-    grads_added(0)
+    grads_one(2)
     input_group(3)
     input_pair(2)
     input_added(1)
+    grads_added(1)
+    grads_two(2)
     input_sum(0)
     input_pair(3)
-    grads_one(2)
-    grads_added(1)
     input_added(2)
     input_sum(1)
-    grads_two(2)
     input_added(3)
     grads_added(2)
     input_sum(2)
@@ -553,16 +550,23 @@
     finish(2)
     for cp in pending + pulls[-2:]:
         cp.wait_send()
-
-
-def copy_out(dx, g1, g2, dx_out, g1_out, g2_out, sem):
-    copies = [pltpu.make_async_copy(dx, dx_out, sem.at[12])]
+    for cp in leaving:
+        cp.wait()
+
+
+def copy_out(dx, g1, g2, dx_out, g1_out, g2_out, dx_v, g1_v, g2_v, sem):
+    steps = [(dx, dx_v, dx_out)]
     for col in range(6):
-        copies.append(pltpu.make_async_copy(g1.at[col], g1_out.at[col], sem.at[2 * col]))
-        copies.append(pltpu.make_async_copy(g2.at[col], g2_out.at[col], sem.at[2 * col + 1]))
-    for cp in copies:
+        steps.append((g1.at[col], g1_v.at[col], g1_out.at[col]))
+        steps.append((g2.at[col], g2_v.at[col], g2_out.at[col]))
+    reads = [pltpu.make_async_copy(a, v, sem.at[0, n]) for n, (a, v, b) in enumerate(steps)]
+    writes = [pltpu.make_async_copy(v, b, sem.at[1, n]) for n, (a, v, b) in enumerate(steps)]
+    for cp in reads:
         cp.start()
-    for cp in copies:
+    for read, write in zip(reads, writes):
+        read.wait()
+        write.start()
+    for cp in writes:
         cp.wait()
 
 
@@ -582,7 +586,7 @@
         kernel,
         out_shape=shapes,
         in_specs=[any_space] * 4 + [smem] * 4,
-        out_specs=(vmem, vmem, vmem),
+        out_specs=(vmem, any_space, any_space),
         scratch_shapes=[
             pltpu.VMEM((128, 12288), BF16),
             pltpu.VMEM((128, 12288), BF16),
@@ -605,6 +609,8 @@
             pltpu.VMEM((6, 4, 128, 128), BF16),
             pltpu.VMEM((3, 4, 128, 128), BF16),
             pltpu.VMEM((3, 4, 128, 128), BF16),
+            pltpu.VMEM((6, 4, 128, 128), BF16),
+            pltpu.VMEM((6, 4, 128, 128), BF16),
             pltpu.VMEM((4, 8, 128, 384), F32),
             pltpu.VMEM((4, 8, 128, 384), BF16),
             pltpu.VMEM((4, 8, 128, 384), BF16),
@@ -613,6 +619,7 @@
             pltpu.VMEM((7, 128, 384), BF16),
             pltpu.VMEM((128, 384), F32),
             pltpu.VMEM((7, 128, 384), BF16),
+            dma((2, 6)),
             pltpu.SemaphoreType.REGULAR((2,)),
             dma((11,)),
             dma((7,)), dma((7,)),
@@ -627,7 +634,7 @@
             dma((24,)), dma((24,)),
             dma((3,)), dma((3,)),
             dma((3,)), dma((3,)),
-            dma((3, 2)), dma((3, 2)),
+            dma((3,)), dma((3,)),
             dma((3, 2, 2)), dma((2, 6)),
             dma((3, 2)), dma((6,)),
             dma((3, 2)), dma((3, 2)),
@@ -642,9 +649,14 @@
     return pl.pallas_call(
         copy_out,
         out_shape=shapes,
-        in_specs=[vmem] * 3,
+        in_specs=[any_space] * 3,
         out_specs=(any_space,) * 3,
-        scratch_shapes=[dma((13,))],
+        scratch_shapes=[
+            pltpu.VMEM((128, 384), BF16),
+            pltpu.VMEM((6, 4, 128, 128), BF16),
+            pltpu.VMEM((6, 4, 128, 128), BF16),
+            dma((2, 13)),
+        ],
     )(*grads)
 
 

time: 115 us -> 113 us (0.983)
    pallas_call x1, Pallas kernels: 111 us -> 109 us  [per_device(): pl.pallas_call(kernel, out_shape=shapes, in_specs=[any_space] * 4 + [smem...]
where the time goes in v4:
time: 113 us
  Pallas kernels  112 us (99%)
    pallas_call x1, Pallas kernels, per_device(): pl.pallas_call(kernel, out_shape=shapes, in_specs=[any_space] * 4 + [smem...  109 us
    pallas_call x1, Pallas kernels, per_device(): pl.pallas_call(copy_out, out_shape=shapes, in_specs=[any_space] * 3, out_...  2.39 us

profile of v4, /device:TPU:64, one launch (start us, length us, event | category | flops | bytes accessed | tf_op | source)
XLA Modules:
  0.0 112.5 jit_solution(2904034420026917713)
XLA Ops:
  0.6 109.5 %shard_map.103 = (bf16[128,384]{1,0:T(8,128)(2,1)}, bf16[6,4,128,128]{3,2,1,0:T(8,128)(2,1)}, bf16[6,4,128,128]{3,2,1,0:T(8,128)(2,1)}) custom-call(bf16[128,12288]{1,0:T(8,128)(2,1)} %x_hbm.1, bf16[128,12288]{1,0:T(8,128)(2,1)} %dy_hbm.1, bf16[6,4,128,128]{3,2,1,0:T(8,128)(2,1)} %w1_hbm.1, bf16[6,4,128,128]{3,2,1,0:T(8,128)(2,1)} %w2_hbm.1, ...), custom_call_target="tpu_custom_call" | custom-call | tf_op jit(solution)/shard_map/pallas_call | solution.py:585
  110.1 2.4 %shard_map.104 = (bf16[128,384]{1,0:T(8,128)(2,1)}, bf16[6,4,128,128]{3,2,1,0:T(8,128)(2,1)}, bf16[6,4,128,128]{3,2,1,0:T(8,128)(2,1)}) custom-call(bf16[128,384]{1,0:T(8,128)(2,1)} %get-tuple-element.6.dx, bf16[6,4,128,128]{3,2,1,0:T(8,128)(2,1)} %get-tuple-element.7.g1, bf16[6,4,128,128]{3,2,1,0:T(8,128)(2,1)} %get-tuple-element.8.g2), custom_call_target="tpu_custom_call" | custom-call | tf_op jit(solution)/shard_map/pallas_call | solution.py:649

commit v5 on v4

--- a/solution.py
+++ b/solution.py
@@ -500,13 +500,13 @@
     relay_y(3)
     forward(2, xp, xn, way_n)
     complete_two(1)
+    act_own(1)
     complete_two(2)
+    act_own(2)
     partner_ready()
     act_other(0)
     act_other(1)
     act_other(2)
-    act_own(1)
-    act_own(2)
     complete_one(0)
     hidden_pass(0)
     activate(0)

time: 113 us -> 113 us (level)
  no operation moved by 1% of the time
where the time goes in v5:
time: 113 us
  Pallas kernels  112 us (99%)
    pallas_call x1, Pallas kernels, per_device(): pl.pallas_call(kernel, out_shape=shapes, in_specs=[any_space] * 4 + [smem...  109 us
    pallas_call x1, Pallas kernels, per_device(): pl.pallas_call(copy_out, out_shape=shapes, in_specs=[any_space] * 3, out_...  2.39 us

profile of v5, /device:TPU:64, one launch (start us, length us, event | category | flops | bytes accessed | tf_op | source)
XLA Modules:
  0.0 112.5 jit_solution(13825994434389754081)
XLA Ops:
  0.6 109.5 %shard_map.103 = (bf16[128,384]{1,0:T(8,128)(2,1)}, bf16[6,4,128,128]{3,2,1,0:T(8,128)(2,1)}, bf16[6,4,128,128]{3,2,1,0:T(8,128)(2,1)}) custom-call(bf16[128,12288]{1,0:T(8,128)(2,1)} %x_hbm.1, bf16[128,12288]{1,0:T(8,128)(2,1)} %dy_hbm.1, bf16[6,4,128,128]{3,2,1,0:T(8,128)(2,1)} %w1_hbm.1, bf16[6,4,128,128]{3,2,1,0:T(8,128)(2,1)} %w2_hbm.1, ...), custom_call_target="tpu_custom_call" | custom-call | tf_op jit(solution)/shard_map/pallas_call | solution.py:585
  110.1 2.4 %shard_map.104 = (bf16[128,384]{1,0:T(8,128)(2,1)}, bf16[6,4,128,128]{3,2,1,0:T(8,128)(2,1)}, bf16[6,4,128,128]{3,2,1,0:T(8,128)(2,1)}) custom-call(bf16[128,384]{1,0:T(8,128)(2,1)} %get-tuple-element.6.dx, bf16[6,4,128,128]{3,2,1,0:T(8,128)(2,1)} %get-tuple-element.7.g1, bf16[6,4,128,128]{3,2,1,0:T(8,128)(2,1)} %get-tuple-element.8.g2), custom_call_target="tpu_custom_call" | custom-call | tf_op jit(solution)/shard_map/pallas_call | solution.py:649
